TPU v7x, 32 devices: a whole 2x2x4 slice. The times are simulated.
32 devices in a mesh: blk: 8 (over y, x, core), pw: 4 (over z).
Axes of the slice: x: 2, y: 2, z: 4, core: 2. Of those that a mesh axis runs over, the one named last changes fastest.
Arguments:
- res_pair: bfloat16 [16384, 12288], P('blk', 'pw'), may hold values from -0.56640625 to 0.56640625
- band_pair: bfloat16 [2048, 12288], P('blk', 'pw'), may hold values from -0.56640625 to 0.56640625
- coulomb: float32 [12288], P('pw'), may hold values from 0.2 to 5
- screening: float32 [2048], P('pw'), may hold values from 0.2 to 5
- val_form: bfloat16 [400, 2048], P(None, 'pw'), may hold values from -2.3125 to 2.3125
- cond_form: bfloat16 [600, 2048], P(None, 'pw'), may hold values from -2.3125 to 2.3125
- res_bands: int32 [3, 16384], P(None, 'blk'), may hold values from 0 to 299, as said below
- band_bands: int32 [3, 2048], P(None, 'blk'), may hold values from 0 to 299, as said below
Outputs:
- kernel: float32 [2, 16384, 256], P(None, ('blk', 'pw'))
Inputs may be any that keep to these rules, and one draw needn't show every extreme that they name: `res_bands`: row 0 holds valence bands below 200, row 1 conduction bands below 300, row 2 k-points below 2. `band_bands`: row 0 holds valence bands below 200, row 1 conduction bands below 300, row 2 k-points below 2.
All inputs are finite; a program needn't handle non-finite values.
Results may differ from a plain program's by a relative error of at most 0.01.
Values may be sent and summed in bfloat16 or wider, within the bound.
A program may use at most 64 MiB of HBM per device.

v0:
```python
import jax
import jax.numpy as jnp
from jax import lax
from jax.sharding import PartitionSpec as P

NV = 200
NC = 300
STEPS = 2


def passed_along(x, axis, by):
    size = lax.axis_size(axis)
    return lax.ppermute(x, axis, [(i, (i + by) % size) for i in range(size)])


def make_density(bands, val_form, cond_form):
    rows_val = bands[2] * NV + bands[0]
    rows_cond = bands[2] * NC + bands[1]
    valence = jnp.take(val_form, rows_val, axis=0).astype(jnp.float32)
    conduct = jnp.take(cond_form, rows_cond, axis=0).astype(jnp.float32)
    return (valence * conduct).astype(jnp.bfloat16)


def contract_rows(left, right):
    return lax.dot_general(
        left, right, (((1,), (1,)), ((), ())), preferred_element_type=jnp.float32
    )


def make_term(res_pair, res_density, vis_weight, vis_screen):

    def term(start, count):
        return 2.0 * contract_rows(res_pair, vis_weight) - contract_rows(res_density, vis_screen)

    return term


def local(res_pair, band_pair, coulomb, screening, val_form, cond_form, res_bands, band_bands):
    res_density = make_density(res_bands, val_form, cond_form)
    band_density = make_density(band_bands, val_form, cond_form)
    weighted = (band_pair.astype(jnp.float32) * coulomb[None, :]).astype(jnp.bfloat16)
    screened = (band_density.astype(jnp.float32) * screening[None, :]).astype(jnp.bfloat16)
    own_rows = res_pair.shape[0] // lax.axis_size("pw")
    own_payload = (weighted, screened)
    payload = own_payload
    pieces = []
    for step_index in range(STEPS):
        payload = passed_along((payload[0], payload[1]), "blk", 1)
        vis_weight, vis_screen = payload
        term = make_term(res_pair, res_density, vis_weight, vis_screen)
        pieces.append(
            lax.psum_scatter(
                term(jnp.int32(0), own_rows * lax.axis_size("pw")),
                "pw",
                scatter_dimension=0,
                tiled=True,
            )
        )
    return jnp.stack(pieces, axis=0)


def solution(mesh):
    return jax.shard_map(
        local,
        mesh=mesh,
        in_specs=(
            P("blk", "pw"),
            P("blk", "pw"),
            P("pw"),
            P("pw"),
            P(None, "pw"),
            P(None, "pw"),
            P(None, "blk"),
            P(None, "blk"),
        ),
        out_specs=P(None, ("blk", "pw"), None),
        check_vma=False,
    )
```

profile of v0, /device:TPU:0, one launch (start us, length us, event | category | flops | bytes accessed | tf_op | source)
XLA Modules:
  0.0 146.9 jit_solution(16945051227161648810)
XLA Ops:
  6.5 0.8 compare_select_fusion.5
  7.4 2.3 %gather_fusion.2 = bf16[256,512]{1,0:T(8,128)(2,1)S(1)} fusion(bf16[400,512]{1,0:T(8,128)(2,1)} %param.12, s32[1024]{0:T(1024)S(1)} %pad_clamp_fusion.1), kind=kCustom, calls=%fused_computation.2 | custom fusion | bytes 525312 | tf_op jit(solution)/shard_map/jit(_take)/gather | solution.py:19
  9.7 1.2 gather_fusion.3
  10.9 0.2 multiply_convert_fusion.2
  11.1 0.5 collective-permute-start.1
  11.6 1.5 %multiply_convert_fusion.1 = bf16[256,3072]{1,0:T(8,128)(2,1)} fusion(bf16[256,3072]{1,0:T(8,128)(2,1)S(1)} %copy-done.2, f32[3072]{0:T(1024)S(1)} %copy-done.4), kind=kLoop, calls=%fused_computation.5 | loop fusion | flops 2359296 | bytes 3158016 | tf_op jit(solution)/shard_map/convert_element_type | solution.py:41
  13.1 2.6 %collective-permute-start = (bf16[256,3072]{1,0:T(8,128)(2,1)}, bf16[256,3072]{1,0:T(8,128)(2,1)}, u32[]{:S(2)}, u32[]{:S(2)}) collective-permute-start(bf16[256,3072]{1,0:T(8,128)(2,1)} %multiply_convert_fusion.1), channel_id=1, source_target_pairs={{0,4},{4,8},{8,12},{12,16},{16,20},{20,24},{24,28},{28,0},{1,5},{5... | collective-permute-start | bytes 4718600 | tf_op jit(solution)/shard_map/ppermute | solution.py:13
  15.8 9.2 %gather_fusion = bf16[2048,512]{1,0:T(8,128)(2,1)} fusion(bf16[400,512]{1,0:T(8,128)(2,1)S(1)} %copy-done.1, s32[2048]{0:T(1024)S(1)} %broadcast_clamp_fusion.1), kind=kCustom, calls=%fused_computation | custom fusion | bytes 4202496 | tf_op jit(solution)/shard_map/jit(_take)/gather | solution.py:19
  25.0 9.2 %gather_fusion.1 = bf16[2048,512]{1,0:T(8,128)(2,1)} fusion(bf16[600,512]{1,0:T(8,128)(2,1)S(1)} %copy-done, s32[2048]{0:T(1024)S(1)} %broadcast_clamp_fusion), kind=kCustom, calls=%fused_computation.1 | custom fusion | bytes 4202496 | tf_op jit(solution)/shard_map/jit(_take)/gather | solution.py:20
  34.1 2.7 %multiply_convert_fusion = bf16[2048,512]{1,0:T(8,128)(2,1)S(1)} fusion(bf16[2048,512]{1,0:T(8,128)(2,1)} %gather_fusion.1, bf16[2048,512]{1,0:T(8,128)(2,1)} %gather_fusion, pred[2048]{0:T(1024)(128)(4,1)S(1)} %get-tuple-element.17, pred[2048]{0:T(1024)(128)(4,1)S(1)} %get-tuple-element.18), kind=kLoop, calls=%fused_computation.4 | loop fusion | flops 6291456 | bytes 6295552 | tf_op jit(solution)/shard_map/convert_element_type | solution.py:21
  36.8 0.7 fusion.4
  37.6 9.9 %fusion.2 = f32[2048,256]{0,1:T(8,128)} fusion(f32[2048,256]{0,1:T(8,128)S(1)} %fusion.4, bf16[256,3072]{1,0:T(8,128)(2,1)} %collective-permute-done, bf16[2048,3072]{1,0:T(8,128)(2,1)} %param.8), kind=kOutput, calls=%fused_computation.10 | convolution fusion | flops 3222274048 | bytes 18350080 | tf_op jit(solution)/shard_map/dot_general | solution.py:25
  47.5 0.0 reduce-scatter.3.cloned.1.call-update
  47.5 0.0 reduce-scatter.5.cloned.1.call-start
  47.5 0.1 collective-permute-start.2
  47.6 1.6 %collective-permute-start.3 = (bf16[256,512]{1,0:T(8,128)(2,1)S(1)}, bf16[256,512]{1,0:T(8,128)(2,1)S(1)}, u32[]{:S(2)}, u32[]{:S(2)}) collective-permute-start(bf16[256,512]{1,0:T(8,128)(2,1)S(1)} %collective-permute-done.1), channel_id=1, source_target_pairs={{0,4},{4,8},{8,12},{12,16},{16,20},{20,24},{24,28},{28,0},{1,5},{5... | collective-permute-start | bytes 786440 | tf_op jit(solution)/shard_map/ppermute | solution.py:13
  49.2 22.1 %collective-permute-done.3 = bf16[256,512]{1,0:T(8,128)(2,1)S(1)} collective-permute-done((bf16[256,512]{1,0:T(8,128)(2,1)S(1)}, bf16[256,512]{1,0:T(8,128)(2,1)S(1)}, u32[]{:S(2)}, u32[]{:S(2)}) %collective-permute-start.3) | collective-permute-done | bytes 262176 | tf_op jit(solution)/shard_map/ppermute | solution.py:13
  71.4 0.7 fusion.5
  72.1 9.4 %fusion.3 = f32[2048,256]{0,1:T(8,128)} fusion(f32[2048,256]{0,1:T(8,128)S(1)} %fusion.5, bf16[256,3072]{1,0:T(8,128)(2,1)S(1)} %collective-permute-done.2, bf16[2048,3072]{1,0:T(8,128)(2,1)} %param.8), kind=kOutput, calls=%fused_computation.11 | convolution fusion | flops 3222274048 | bytes 18350080 | tf_op jit(solution)/shard_map/dot_general | solution.py:25
  81.5 0.0 reduce-scatter.5.cloned.1.call-update
  81.6 10.3 %reduce-scatter.3.cloned.1.call-done = f32[512,256]{0,1:T(8,128)} async-done(((f32[2048,256]{0,1:T(8,128)}), f32[512,256]{0,1:T(8,128)}) %reduce-scatter.3.cloned.1.call-update) | async-done | bytes 524304 | tf_op jit(solution)/shard_map/reduce_scatter | solution.py:52
  91.8 45.6 %reduce-scatter.5.cloned.1.call-done = f32[512,256]{0,1:T(8,128)} async-done(((f32[2048,256]{0,1:T(8,128)}), f32[512,256]{0,1:T(8,128)}) %reduce-scatter.5.cloned.1.call-update) | async-done | bytes 524304 | tf_op jit(solution)/shard_map/reduce_scatter | solution.py:52
  137.5 1.3 pad_maximum_fusion
  138.7 1.3 copy.14
  (23 shorter events, 0.1 us)
Async XLA Ops:
  6.5 3.1 %copy-start = (bf16[600,512]{1,0:T(8,128)(2,1)S(1)}, bf16[600,512]{1,0:T(8,128)(2,1)}, u32[]{:S(2)}) copy-start(bf16[600,512]{1,0:T(8,128)(2,1)} %param.13) | copy-start | bytes 1843204
  6.5 85.3 %reduce-scatter.3.cloned.1.call-start = ((), (), s32[]{:S(2)}) async-start(), calls=%async_computation.2 | async-start | bytes 2621440 | tf_op jit(solution)/shard_map/reduce_scatter | solution.py:52
  7.4 3.5 %copy-start.5 = (f32[512]{0:T(512)S(1)}, f32[512]{0:T(512)}, u32[]{:S(2)}) copy-start(f32[512]{0:T(512)} %param.11) | copy-start | bytes 6148
  9.7 1.9 %copy-start.2 = (bf16[256,3072]{1,0:T(8,128)(2,1)S(1)}, bf16[256,3072]{1,0:T(8,128)(2,1)}, u32[]{:S(2)}) copy-start(bf16[256,3072]{1,0:T(8,128)(2,1)} %param.9) | copy-start | bytes 4718596
  9.7 1.9 %copy-start.4 = (f32[3072]{0:T(1024)S(1)}, f32[3072]{0:T(1024)}, u32[]{:S(2)}) copy-start(f32[3072]{0:T(1024)} %param.10) | copy-start | bytes 36868
  10.9 4.8 %copy-start.3 = (s32[3,2048]{1,0:T(4,128)S(1)}, s32[3,2048]{1,0:T(4,128)}, u32[]{:S(2)}) copy-start(s32[3,2048]{1,0:T(4,128)} %param.14) | copy-start | bytes 73732
  10.9 4.9 %copy-start.1 = (bf16[400,512]{1,0:T(8,128)(2,1)S(1)}, bf16[400,512]{1,0:T(8,128)(2,1)}, u32[]{:S(2)}) copy-start(bf16[400,512]{1,0:T(8,128)(2,1)} %param.12) | copy-start | bytes 1228804
  11.1 25.7 %collective-permute-start.1 = (bf16[256,512]{1,0:T(8,128)(2,1)S(1)}, bf16[256,512]{1,0:T(8,128)(2,1)S(1)}, u32[]{:S(2)}, u32[]{:S(2)}) collective-permute-start(bf16[256,512]{1,0:T(8,128)(2,1)S(1)} %multiply_convert_fusion.2), channel_id=1, source_target_pairs={{0,4},{4,8},{8,12},{12,16},{16,20},{20,24},{24,28},{28,0},{1,5},{5... | collective-permute-start | bytes 786440 | tf_op jit(solution)/shard_map/ppermute | solution.py:13
  13.1 24.5 %collective-permute-start = (bf16[256,3072]{1,0:T(8,128)(2,1)}, bf16[256,3072]{1,0:T(8,128)(2,1)}, u32[]{:S(2)}, u32[]{:S(2)}) collective-permute-start(bf16[256,3072]{1,0:T(8,128)(2,1)} %multiply_convert_fusion.1), channel_id=1, source_target_pairs={{0,4},{4,8},{8,12},{12,16},{16,20},{20,24},{24,28},{28,0},{1,5},{5... | collective-permute-start | bytes 4718600 | tf_op jit(solution)/shard_map/ppermute | solution.py:13
  47.5 90.0 %reduce-scatter.5.cloned.1.call-start = ((), (), s32[]{:S(2)}) async-start(), calls=%async_computation.3 | async-start | bytes 2621440 | tf_op jit(solution)/shard_map/reduce_scatter | solution.py:52
  47.5 24.6 %collective-permute-start.2 = (bf16[256,3072]{1,0:T(8,128)(2,1)}, bf16[256,3072]{1,0:T(8,128)(2,1)S(1)}, u32[]{:S(2)}, u32[]{:S(2)}) collective-permute-start(bf16[256,3072]{1,0:T(8,128)(2,1)} %collective-permute-done), channel_id=1, source_target_pairs={{0,4},{4,8},{8,12},{12,16},{16,20},{20,24},{24,28},{28,0},{1,5},{5... | collective-permute-start | bytes 4718600 | tf_op jit(solution)/shard_map/ppermute | solution.py:13
  47.6 23.7 %collective-permute-start.3 = (bf16[256,512]{1,0:T(8,128)(2,1)S(1)}, bf16[256,512]{1,0:T(8,128)(2,1)S(1)}, u32[]{:S(2)}, u32[]{:S(2)}) collective-permute-start(bf16[256,512]{1,0:T(8,128)(2,1)S(1)} %collective-permute-done.1), channel_id=1, source_target_pairs={{0,4},{4,8},{8,12},{12,16},{16,20},{20,24},{24,28},{28,0},{1,5},{5... | collective-permute-start | bytes 786440 | tf_op jit(solution)/shard_map/ppermute | solution.py:13
Sparse Core Ops, SparseCore 0:
  47.6 44.1 reduce-scatter.2
  94.2 43.1 reduce-scatter.4
where the time goes:
time: 147 us
  waiting for transfers between devices  78.1 us (53%)
  local copies, waits for them, and re-layouts  23.1 us (16%)
  matrix products  20.8 us (14%)
  between operations  13.6 us (9%)
  other arithmetic  6.53 us (4%)
  starting transfers between devices  4.81 us (3%)
    reduce_scatter x2, waiting for transfers between devices, local(): lax.psum_scatter(term(jnp.int32(0), own_rows * lax.axis_size('pw')), 'pw'...  55.9 us
    ppermute x4, waiting for transfers between devices, passed_along(): return lax.ppermute(x, axis, [(i, (i + by) % size) for i in range(size)])  22.2 us
    dot_general x4, matrix products, contract_rows(): lax.dot_general(left, right, (((1,), (1,)), ((), ())), preferred_element_...  20.8 us
    gather x2, local copies, waits for them, and re-layouts, make_density(): valence = jnp.take(val_form, rows_val, axis=0).astype(jnp.float32)  11.4 us
    gather x2, local copies, waits for them, and re-layouts, make_density(): conduct = jnp.take(cond_form, rows_cond, axis=0).astype(jnp.float32)  10.3 us
    ppermute x4, starting transfers between devices, passed_along(): return lax.ppermute(x, axis, [(i, (i + by) % size) for i in range(size)])  4.77 us
  transfers between devices with their start and end apart: 6, of which 3 were waited for; matrix products, arithmetic and copies ran while one was open for 23% of the time, Pallas kernels for 0%

commit v1 on v0

v1 whole, which is shorter than its diff:
```python
import functools

import jax
import jax.numpy as jnp
from jax import lax
from jax.experimental import pallas as pl
from jax.experimental.pallas import tpu as pltpu
from jax.sharding import PartitionSpec as P

NV = 200
NC = 300
STEPS = 2
LANES = 128
GROUP = 256
MESH = pl.DeviceIdType.MESH


def rounded_up(count, unit):
    return (count + unit - 1) // unit * unit


def kernel(
    n_blk, n_pw, n_val,
    res_hbm, band_ref, coul_ref, scr_ref, forms_ref, res_bands, band_bands, out_ref,
    res, res_sem, dens, bidx, idx_in, wgt, rhs, rhs_scr, part, up_in, dn_in, up_out, dn_out, final,
    idx_send, idx_recv, near_send, far_send, fwd_send, rhs_recv,
    up_send, up_recv, dn_send, dn_recv,
):
    chunks, rows = wgt.shape[0], wgt.shape[1]
    own_rows = out_ref.shape[1]
    me = lax.axis_index("blk")
    w = lax.axis_index("pw")
    even = lax.rem(me, 2) == 0
    one_on, two_on = lax.rem(me + 1, n_blk), lax.rem(me + 2, n_blk)
    one_back, two_back = lax.rem(me + n_blk - 1, n_blk), lax.rem(me + n_blk - 2, n_blk)

    load = pltpu.make_async_copy(res_hbm, res, res_sem)
    load.start()

    barrier = pltpu.get_barrier_semaphore()
    for other in (one_on, two_on, one_back, two_back):
        pl.semaphore_signal(barrier, inc=1, device_id=(other, w), device_id_type=MESH)

    @pl.when(w > 0)
    def _():
        pl.semaphore_signal(barrier, inc=1, device_id=(me, w - 1), device_id_type=MESH)

    @pl.when(w < n_pw - 1)
    def _():
        pl.semaphore_signal(barrier, inc=1, device_id=(me, w + 1), device_id_type=MESH)

    peers = 4 + jnp.where(w > 0, 1, 0) + jnp.where(w < n_pw - 1, 1, 0)
    pl.semaphore_wait(barrier, peers)

    def remote(src, dst, send, recv, blk, pw):
        return pltpu.make_async_remote_copy(
            src_ref=src, dst_ref=dst, send_sem=send, recv_sem=recv,
            device_id=(blk, pw), device_id_type=MESH,
        )

    def send_index(slot, target):
        return remote(bidx, idx_in.at[slot], idx_send.at[slot], idx_recv.at[slot], target, w)

    def send_near(c):
        return remote(wgt.at[c], rhs.at[c, 0], near_send.at[c], rhs_recv.at[c, 0], one_on, w)

    def send_far(c):
        return remote(wgt.at[c], rhs.at[c, 1], far_send.at[c], rhs_recv.at[c, 1], two_on, w)

    def forward(c):
        return remote(rhs.at[c, 0], rhs.at[c, 1], fwd_send.at[c], rhs_recv.at[c, 1], one_on, w)

    def send_up(c, q):
        return remote(up_out.at[c, q], up_in.at[c, q], up_send.at[c, q], up_recv.at[c, q], me, w + 1)

    def send_dn(c, q):
        return remote(dn_out.at[c, q], dn_in.at[c, q], dn_send.at[c, q], dn_recv.at[c, q], me, w - 1)

    bidx[...] = jnp.zeros_like(bidx)
    bidx[0:1, :] = band_bands[2:3, :] * NV + band_bands[0:1, :]
    bidx[1:2, :] = band_bands[2:3, :] * NC + band_bands[1:2, :]
    send_index(0, one_on).start()
    send_index(1, two_on).start()

    @pl.loop(0, chunks)
    def _(c):
        block = band_ref[pl.ds(pl.multiple_of(c * rows, rows), rows), :].astype(jnp.float32)
        wgt[c] = (block * (2.0 * coul_ref[...])).astype(jnp.bfloat16)
        send_near(c).start()

        @pl.when(even)
        def _():
            send_far(c).start()

    val_depth = rounded_up(n_val, LANES)
    cond_from = n_val // LANES * LANES
    cond_depth = forms_ref.shape[0] - cond_from

    def one_hot(row, depth):
        column = jnp.concatenate(
            [
                jnp.broadcast_to(row[:, h * LANES:(h + 1) * LANES], (LANES, LANES)).T
                for h in range(GROUP // LANES)
            ],
            axis=0,
        )
        lane = lax.broadcasted_iota(jnp.int32, (GROUP, LANES), 1)
        return jnp.concatenate(
            [
                jnp.where(column == lane + start, 1.0, 0.0).astype(jnp.bfloat16)
                for start in range(0, depth, LANES)
            ],
            axis=1,
        )

    def density(val_row, cond_row):
        valence = jnp.dot(
            one_hot(val_row, val_depth), forms_ref[:val_depth, :], preferred_element_type=jnp.float32
        )
        conduct = jnp.dot(
            one_hot(cond_row + (n_val - cond_from), cond_depth), forms_ref[cond_from:, :],
            preferred_element_type=jnp.float32,
        )
        return (valence * conduct).astype(jnp.bfloat16)

    @pl.loop(0, dens.shape[0] // GROUP)
    def _(g):
        at = pl.ds(pl.multiple_of(g * GROUP, GROUP), GROUP)
        point = res_bands[2:3, at]
        dens[at, :] = density(point * NV + res_bands[0:1, at], point * NC + res_bands[1:2, at])

    for slot, target in ((0, one_on), (1, two_on)):
        send_index(slot, target).wait_recv()
        for g in range(chunks * rows // GROUP):
            at = slice(g * GROUP, (g + 1) * GROUP)
            block = density(idx_in[slot, 0:1, at], idx_in[slot, 1:2, at])
            block = (block.astype(jnp.float32) * (-scr_ref[...])).astype(jnp.bfloat16)
            for h in range(GROUP // rows):
                rhs_scr[g * (GROUP // rows) + h, slot] = block[h * rows:(h + 1) * rows, :]

    load.wait()

    def multiply(c):
        send_near(c).wait_recv()

        @pl.when(even)
        def _():
            forward(c).start()

        send_far(c).wait_recv()
        weighted = rhs[c].reshape(2 * rows, rhs.shape[3])
        screened = rhs_scr[c].reshape(2 * rows, rhs_scr.shape[3])

        @pl.loop(0, n_pw)
        def _(j):
            q = jnp.where(2 * w < n_pw, n_pw - 1 - j, j)
            at = pl.ds(pl.multiple_of(q * own_rows, own_rows), own_rows)
            contract = (((1,), (1,)), ((), ()))
            term = lax.dot_general(
                res[at, :], weighted, contract, preferred_element_type=jnp.float32
            ) + lax.dot_general(
                dens[at, :], screened, contract, preferred_element_type=jnp.float32
            )
            part[lax.rem(c, 2), q] = term

            @pl.when(jnp.logical_and(w == 0, q > 0))
            def _():
                up_out[c, q] = term.astype(jnp.bfloat16)
                send_up(c, q).start()

            @pl.when(jnp.logical_and(w == n_pw - 1, q < n_pw - 1))
            def _():
                dn_out[c, q] = term.astype(jnp.bfloat16)
                send_dn(c, q).start()

    def relay(c):
        slot = lax.rem(c, 2)

        def upward():
            @pl.when(w > 0)
            def _():
                @pl.loop(0, n_pw - 1 - w)
                def _(j):
                    q = n_pw - 1 - j
                    send_up(c, q).wait_recv()
                    total = part[slot, q] + up_in[c, q].astype(jnp.float32)
                    up_out[c, q] = total.astype(jnp.bfloat16)
                    send_up(c, q).start()

        def downward():
            @pl.when(w < n_pw - 1)
            def _():
                @pl.loop(0, w)
                def _(q):
                    send_dn(c, q).wait_recv()
                    total = part[slot, q] + dn_in[c, q].astype(jnp.float32)
                    dn_out[c, q] = total.astype(jnp.bfloat16)
                    send_dn(c, q).start()

        @pl.when(2 * w < n_pw)
        def _():
            upward()
            downward()

        @pl.when(2 * w >= n_pw)
        def _():
            downward()
            upward()

        final[c] = part[slot, w]

        @pl.when(w > 0)
        def _():
            send_up(c, w).wait_recv()
            final[c] += up_in[c, w].astype(jnp.float32)

        @pl.when(w < n_pw - 1)
        def _():
            send_dn(c, w).wait_recv()
            final[c] += dn_in[c, w].astype(jnp.float32)

    @pl.loop(0, chunks)
    def _(c):
        multiply(c)

        @pl.when(c > 0)
        def _():
            relay(c - 1)

    relay(chunks - 1)

    for c in range(chunks):
        for s in range(STEPS):
            out_ref[s, :, c * rows:(c + 1) * rows] = final[c][:, s * rows:(s + 1) * rows]

    send_index(0, one_on).wait_send()
    send_index(1, two_on).wait_send()

    @pl.loop(0, chunks)
    def _(c):
        send_near(c).wait_send()

        @pl.when(even)
        def _():
            send_far(c).wait_send()
            forward(c).wait_send()

        @pl.when(w < n_pw - 1)
        def _():
            @pl.loop(w + 1, n_pw)
            def _(q):
                send_up(c, q).wait_send()

        @pl.when(w > 0)
        def _():
            @pl.loop(0, w)
            def _(q):
                send_dn(c, q).wait_send()


def local(n_blk, n_pw, res_pair, band_pair, coulomb, screening, val_form, cond_form, res_bands, band_bands):
    n_res, depth = res_pair.shape
    n_band = band_pair.shape[0]
    width = val_form.shape[1]
    n_val, n_cond = val_form.shape[0], cond_form.shape[0]
    chunks = 4 if n_pw <= 4 else 2
    rows = n_band // chunks
    own_rows = n_res // n_pw
    spare = rounded_up(n_val + n_cond, LANES) - n_val - n_cond
    forms = jnp.concatenate([val_form, cond_form, jnp.zeros((spare, width), val_form.dtype)], axis=0)
    bf16, f32, i32 = jnp.bfloat16, jnp.float32, jnp.int32
    dma = pltpu.SemaphoreType.DMA
    vmem = pl.BlockSpec(memory_space=pltpu.VMEM)
    return pl.pallas_call(
        functools.partial(kernel, n_blk, n_pw, n_val),
        out_shape=jax.ShapeDtypeStruct((STEPS, own_rows, n_band), f32),
        in_specs=[pl.BlockSpec(memory_space=pl.ANY)] + [vmem] * 6,
        out_specs=vmem,
        scratch_shapes=[
            pltpu.VMEM((n_res, depth), bf16),
            dma(()),
            pltpu.VMEM((n_res, width), bf16),
            pltpu.VMEM((8, n_band), i32),
            pltpu.VMEM((2, 8, n_band), i32),
            pltpu.VMEM((chunks, rows, depth), bf16),
            pltpu.VMEM((chunks, 2, rows, depth), bf16),
            pltpu.VMEM((chunks, 2, rows, width), bf16),
            pltpu.VMEM((2, n_pw, own_rows, 2 * rows), f32),
            pltpu.VMEM((chunks, n_pw, own_rows, 2 * rows), bf16),
            pltpu.VMEM((chunks, n_pw, own_rows, 2 * rows), bf16),
            pltpu.VMEM((chunks, n_pw, own_rows, 2 * rows), bf16),
            pltpu.VMEM((chunks, n_pw, own_rows, 2 * rows), bf16),
            pltpu.VMEM((chunks, own_rows, 2 * rows), f32),
            dma((2,)),
            dma((2,)),
            dma((chunks,)),
            dma((chunks,)),
            dma((chunks,)),
            dma((chunks, 2)),
            dma((chunks, n_pw)),
            dma((chunks, n_pw)),
            dma((chunks, n_pw)),
            dma((chunks, n_pw)),
        ],
        compiler_params=pltpu.CompilerParams(
            collective_id=0, has_side_effects=True, vmem_limit_bytes=56 * 1024 * 1024
        ),
        cost_estimate=pl.CostEstimate(
            flops=2 * STEPS * n_res * n_band * (depth + width),
            bytes_accessed=2 * n_res * depth,
            transcendentals=0,
        ),
        name="kernel_blocks",
    )(res_pair, band_pair, coulomb[None, :], screening[None, :], forms, res_bands, band_bands)


def solution(mesh):
    return jax.shard_map(
        functools.partial(local, mesh.shape["blk"], mesh.shape["pw"]),
        mesh=mesh,
        in_specs=(
            P("blk", "pw"),
            P("blk", "pw"),
            P("pw"),
            P("pw"),
            P(None, "pw"),
            P(None, "pw"),
            P(None, "blk"),
            P(None, "blk"),
        ),
        out_specs=P(None, ("blk", "pw"), None),
        check_vma=False,
    )
```

time: 147 us -> 79.2 us (0.54)
  waiting for transfers between devices: 78.1 us -> 0 us
  Pallas kernels: 0 us -> 74.2 us
  matrix products: 20.8 us -> 0 us
  local copies, waits for them, and re-layouts: 23.1 us -> 2.34 us
  between operations: 13.6 us -> 0.01 us
  starting transfers between devices: 4.81 us -> 0 us
  other arithmetic: 6.53 us -> 2.44 us
    pallas_call x0 -> x1, Pallas kernels: none -> 74.2 us  [local(): pl.pallas_call(functools.partial(kernel, n_blk, n_pw, n_val), out_shape=j...]
    reduce_scatter x2 -> x0, waiting for transfers between devices: 55.9 us -> none  [local(): lax.psum_scatter(term(jnp.int32(0), own_rows * lax.axis_size('pw')), 'pw'...]
    ppermute x4 -> x0, waiting for transfers between devices: 22.2 us -> none  [passed_along(): return lax.ppermute(x, axis, [(i, (i + by) % size) for i in range(size)])]
    gather x4 -> x0, local copies, waits for them, and re-layouts: 21.8 us -> none  [the longest x2 11.4 us: make_density(): valence = jnp.take(val_form, rows_val, axis=0).astype(jnp.float32)]
    dot_general x4 -> x0, matrix products: 20.8 us -> none  [contract_rows(): lax.dot_general(left, right, (((1,), (1,)), ((), ())), preferred_element_...]
    ppermute x4 -> x0, starting transfers between devices: 4.77 us -> none  [passed_along(): return lax.ppermute(x, axis, [(i, (i + by) % size) for i in range(size)])]
    convert_element_type x3 -> x0, other arithmetic: 4.38 us -> none  [the longest x1 2.69 us: make_density(): return (valence * conduct).astype(jnp.bfloat16)]
    concatenate x0 -> x1, other arithmetic: none -> 2.44 us  [local(): jnp.concatenate([val_form, cond_form, jnp.zeros((spare, width), val_form....]
  transfers between devices with their start and end apart: 6 -> 0, of which waited for: 3 -> 0; matrix products, arithmetic and copies ran while one was open for 23% -> 0% of each run, Pallas kernels for 0% -> 0%
where the time goes in v1:
time: 79.2 us; the launch traced here: 79 us
  Pallas kernels  74.2 us (94%)
  other arithmetic  2.44 us (3%)
  local copies, waits for them, and re-layouts  2.34 us (3%)
    pallas_call x1, Pallas kernels, local(): pl.pallas_call(functools.partial(kernel, n_blk, n_pw, n_val), out_shape=j...  74.2 us
    concatenate x1, other arithmetic, local(): jnp.concatenate([val_form, cond_form, jnp.zeros((spare, width), val_form....  2.44 us
    unnamed x1, local copies, waits for them, and re-layouts  2.26 us

profile of v1, /device:TPU:0, one launch (start us, length us, event | category | flops | bytes accessed | tf_op | source)
XLA Modules:
  0.0 79.0 jit_solution(4214226063613145221)
XLA Ops:
  0.0 0.1 pad.2.clone
  0.1 2.4 %maximum_maximum_fusion.forms_ref = bf16[1024,512]{1,0:T(8,128)(2,1)} fusion(bf16[600,512]{1,0:T(8,128)(2,1)} %param.13, bf16[400,512]{1,0:T(8,128)(2,1)} %param.12, bf16[1024]{0:T(1024)(128)(2,1)S(1)} %pad.2.clone), kind=kLoop, calls=%fused_computation | loop fusion | flops 3145728 | bytes 2074624 | tf_op jit(solution)/shard_map/concatenate | solution.py:270
  2.5 74.2 %kernel_blocks.1 = f32[2,512,256]{2,1,0:T(8,128)} custom-call(bf16[2048,3072]{1,0:T(8,128)(2,1)} %res_hbm.1, bf16[256,3072]{1,0:T(8,128)(2,1)} %band_ref.1, f32[1,3072]{1,0:T(1,128)} %bitcast.2, f32[1,512]{1,0:T(1,128)} %bitcast.3, bf16[1024,512]{1,0:T(8,128)(2,1)} %maximum_maximum_fusion.forms_ref, s32[3,2048]{1,0:T(4,128)} %res_bands.1, s32[3,256]{1,0:T(4,128)} %band_bands.1), custom_call_target="tpu_custom_call" | custom-call | flops 7516192768 | bytes 12582912 | tf_op jit(solution)/shard_map/kernel_blocks/pallas_call | solution.py:274
  76.7 2.3 %copy.10 = f32[2,512,256]{2,1,0:T(8,128)} copy(f32[2,512,256]{2,1,0:T(8,128)} %kernel_blocks.1) | data formatting | bytes 2097152
  (1 shorter events, 0.0 us)

commit v2 on v1

--- a/solution.py
+++ b/solution.py
@@ -20,9 +20,9 @@
 
 
 def kernel(
-    n_blk, n_pw, n_val,
-    res_hbm, band_ref, coul_ref, scr_ref, forms_ref, res_bands, band_bands, out_ref,
-    res, res_sem, dens, bidx, idx_in, wgt, rhs, rhs_scr, part, up_in, dn_in, up_out, dn_out, final,
+    n_blk, n_pw,
+    res_hbm, band_ref, coul_ref, scr_ref, val_form, cond_form, res_bands, band_bands, out_ref,
+    res, res_sem, val_pad, cond_pad, dens, bidx, idx_in, wgt, rhs, rhs_scr, part, up_in, dn_in, up_out, dn_out, final,
     idx_send, idx_recv, near_send, far_send, fwd_send, rhs_recv,
     up_send, up_recv, dn_send, dn_recv,
 ):
@@ -62,13 +62,13 @@
         return remote(bidx, idx_in.at[slot], idx_send.at[slot], idx_recv.at[slot], target, w)
 
     def send_near(c):
-        return remote(wgt.at[c], rhs.at[c, 0], near_send.at[c], rhs_recv.at[c, 0], one_on, w)
+        return remote(wgt.at[c], rhs.at[0, c], near_send.at[c], rhs_recv.at[0, c], one_on, w)
 
     def send_far(c):
-        return remote(wgt.at[c], rhs.at[c, 1], far_send.at[c], rhs_recv.at[c, 1], two_on, w)
+        return remote(wgt.at[c], rhs.at[1, c], far_send.at[c], rhs_recv.at[1, c], two_on, w)
 
     def forward(c):
-        return remote(rhs.at[c, 0], rhs.at[c, 1], fwd_send.at[c], rhs_recv.at[c, 1], one_on, w)
+        return remote(rhs.at[0, c], rhs.at[1, c], fwd_send.at[c], rhs_recv.at[1, c], one_on, w)
 
     def send_up(c, q):
         return remote(up_out.at[c, q], up_in.at[c, q], up_send.at[c, q], up_recv.at[c, q], me, w + 1)
@@ -92,9 +92,9 @@
         def _():
             send_far(c).start()
 
-    val_depth = rounded_up(n_val, LANES)
-    cond_from = n_val // LANES * LANES
-    cond_depth = forms_ref.shape[0] - cond_from
+    for form, padded in ((val_form, val_pad), (cond_form, cond_pad)):
+        spare = jnp.zeros((padded.shape[0] - form.shape[0], form.shape[1]), jnp.float32)
+        padded[...] = jnp.concatenate([form[...].astype(jnp.float32), spare], axis=0).astype(padded.dtype)
 
     def one_hot(row, depth):
         column = jnp.concatenate(
@@ -115,11 +115,10 @@
 
     def density(val_row, cond_row):
         valence = jnp.dot(
-            one_hot(val_row, val_depth), forms_ref[:val_depth, :], preferred_element_type=jnp.float32
+            one_hot(val_row, val_pad.shape[0]), val_pad[...], preferred_element_type=jnp.float32
         )
         conduct = jnp.dot(
-            one_hot(cond_row + (n_val - cond_from), cond_depth), forms_ref[cond_from:, :],
-            preferred_element_type=jnp.float32,
+            one_hot(cond_row, cond_pad.shape[0]), cond_pad[...], preferred_element_type=jnp.float32
         )
         return (valence * conduct).astype(jnp.bfloat16)
 
@@ -136,20 +135,40 @@
             block = density(idx_in[slot, 0:1, at], idx_in[slot, 1:2, at])
             block = (block.astype(jnp.float32) * (-scr_ref[...])).astype(jnp.bfloat16)
             for h in range(GROUP // rows):
-                rhs_scr[g * (GROUP // rows) + h, slot] = block[h * rows:(h + 1) * rows, :]
+                rhs_scr[slot, g * (GROUP // rows) + h] = block[h * rows:(h + 1) * rows, :]
 
     load.wait()
 
+    half = chunks // 2
+
+    def parts_of(c):
+        slot, unit = c // half, 2 * (c % half)
+        return (
+            (jnp.where(even, 0, slot), jnp.where(even, c, unit)),
+            (jnp.where(even, 1, slot), jnp.where(even, c, unit + 1)),
+        )
+
+    def landed(slot, unit):
+        remote(wgt.at[0], rhs.at[slot, unit], near_send.at[0], rhs_recv.at[slot, unit], one_on, w).wait_recv()
+
+    def packed(term):
+        if 2 * rows >= LANES:
+            return term
+        fold = LANES // (2 * rows)
+        tall = own_rows // fold
+        return jnp.concatenate([term[f * tall:(f + 1) * tall] for f in range(fold)], axis=1)
+
     def multiply(c):
-        send_near(c).wait_recv()
+        first, second = parts_of(c)
+        landed(*first)
 
         @pl.when(even)
         def _():
             forward(c).start()
 
-        send_far(c).wait_recv()
-        weighted = rhs[c].reshape(2 * rows, rhs.shape[3])
-        screened = rhs_scr[c].reshape(2 * rows, rhs_scr.shape[3])
+        landed(*second)
+        weighted = jnp.concatenate([rhs[first], rhs[second]], axis=0)
+        screened = jnp.concatenate([rhs_scr[first], rhs_scr[second]], axis=0)
 
         @pl.loop(0, n_pw)
         def _(j):
@@ -161,6 +180,7 @@
             ) + lax.dot_general(
                 dens[at, :], screened, contract, preferred_element_type=jnp.float32
             )
+            term = packed(term)
             part[lax.rem(c, 2), q] = term
 
             @pl.when(jnp.logical_and(w == 0, q > 0))
@@ -173,41 +193,46 @@
                 dn_out[c, q] = term.astype(jnp.bfloat16)
                 send_dn(c, q).start()
 
-    def relay(c):
-        slot = lax.rem(c, 2)
-
-        def upward():
-            @pl.when(w > 0)
-            def _():
-                @pl.loop(0, n_pw - 1 - w)
-                def _(j):
-                    q = n_pw - 1 - j
-                    send_up(c, q).wait_recv()
-                    total = part[slot, q] + up_in[c, q].astype(jnp.float32)
-                    up_out[c, q] = total.astype(jnp.bfloat16)
-                    send_up(c, q).start()
-
-        def downward():
-            @pl.when(w < n_pw - 1)
-            def _():
-                @pl.loop(0, w)
-                def _(q):
-                    send_dn(c, q).wait_recv()
-                    total = part[slot, q] + dn_in[c, q].astype(jnp.float32)
-                    dn_out[c, q] = total.astype(jnp.bfloat16)
-                    send_dn(c, q).start()
-
+    def upward(c):
+        @pl.when(w > 0)
+        def _():
+            @pl.loop(0, n_pw - 1 - w)
+            def _(j):
+                q = n_pw - 1 - j
+                send_up(c, q).wait_recv()
+                total = part[lax.rem(c, 2), q] + up_in[c, q].astype(jnp.float32)
+                up_out[c, q] = total.astype(jnp.bfloat16)
+                send_up(c, q).start()
+
+    def downward(c):
+        @pl.when(w < n_pw - 1)
+        def _():
+            @pl.loop(0, w)
+            def _(q):
+                send_dn(c, q).wait_recv()
+                total = part[lax.rem(c, 2), q] + dn_in[c, q].astype(jnp.float32)
+                dn_out[c, q] = total.astype(jnp.bfloat16)
+                send_dn(c, q).start()
+
+    def relay_near_end(c):
         @pl.when(2 * w < n_pw)
         def _():
-            upward()
-            downward()
+            upward(c)
 
         @pl.when(2 * w >= n_pw)
         def _():
-            downward()
-            upward()
-
-        final[c] = part[slot, w]
+            downward(c)
+
+    def relay_rest(c):
+        @pl.when(2 * w < n_pw)
+        def _():
+            downward(c)
+
+        @pl.when(2 * w >= n_pw)
+        def _():
+            upward(c)
+
+        final[c] = part[lax.rem(c, 2), w]
 
         @pl.when(w > 0)
         def _():
@@ -222,16 +247,35 @@
     @pl.loop(0, chunks)
     def _(c):
         multiply(c)
+        relay_near_end(c)
 
         @pl.when(c > 0)
         def _():
-            relay(c - 1)
-
-    relay(chunks - 1)
-
-    for c in range(chunks):
-        for s in range(STEPS):
-            out_ref[s, :, c * rows:(c + 1) * rows] = final[c][:, s * rows:(s + 1) * rows]
+            relay_rest(c - 1)
+
+    relay_rest(chunks - 1)
+
+    tall = final.shape[1]
+
+    def write(c, place):
+        for f in range(own_rows // tall):
+            block = final[c][:, f * 2 * rows:(f + 1) * 2 * rows]
+            for h in range(2):
+                s, unit = place[h]
+                out_ref[s, f * tall:(f + 1) * tall, unit * rows:(unit + 1) * rows] = (
+                    block[:, h * rows:(h + 1) * rows]
+                )
+
+    @pl.when(even)
+    def _():
+        for c in range(chunks):
+            write(c, ((0, c), (1, c)))
+
+    @pl.when(jnp.logical_not(even))
+    def _():
+        for c in range(chunks):
+            slot, unit = c // half, 2 * (c % half)
+            write(c, ((slot, unit), (slot, unit + 1)))
 
     send_index(0, one_on).wait_send()
     send_index(1, two_on).wait_send()
@@ -266,37 +310,39 @@
     chunks = 4 if n_pw <= 4 else 2
     rows = n_band // chunks
     own_rows = n_res // n_pw
-    spare = rounded_up(n_val + n_cond, LANES) - n_val - n_cond
-    forms = jnp.concatenate([val_form, cond_form, jnp.zeros((spare, width), val_form.dtype)], axis=0)
+    fold = max(1, LANES // (2 * rows))
+    tall, wide = own_rows // fold, 2 * rows * fold
     bf16, f32, i32 = jnp.bfloat16, jnp.float32, jnp.int32
     dma = pltpu.SemaphoreType.DMA
     vmem = pl.BlockSpec(memory_space=pltpu.VMEM)
     return pl.pallas_call(
-        functools.partial(kernel, n_blk, n_pw, n_val),
+        functools.partial(kernel, n_blk, n_pw),
         out_shape=jax.ShapeDtypeStruct((STEPS, own_rows, n_band), f32),
-        in_specs=[pl.BlockSpec(memory_space=pl.ANY)] + [vmem] * 6,
+        in_specs=[pl.BlockSpec(memory_space=pl.ANY)] + [vmem] * 7,
         out_specs=vmem,
         scratch_shapes=[
             pltpu.VMEM((n_res, depth), bf16),
             dma(()),
+            pltpu.VMEM((rounded_up(n_val, LANES), width), bf16),
+            pltpu.VMEM((rounded_up(n_cond, LANES), width), bf16),
             pltpu.VMEM((n_res, width), bf16),
             pltpu.VMEM((8, n_band), i32),
             pltpu.VMEM((2, 8, n_band), i32),
             pltpu.VMEM((chunks, rows, depth), bf16),
-            pltpu.VMEM((chunks, 2, rows, depth), bf16),
-            pltpu.VMEM((chunks, 2, rows, width), bf16),
-            pltpu.VMEM((2, n_pw, own_rows, 2 * rows), f32),
-            pltpu.VMEM((chunks, n_pw, own_rows, 2 * rows), bf16),
-            pltpu.VMEM((chunks, n_pw, own_rows, 2 * rows), bf16),
-            pltpu.VMEM((chunks, n_pw, own_rows, 2 * rows), bf16),
-            pltpu.VMEM((chunks, n_pw, own_rows, 2 * rows), bf16),
-            pltpu.VMEM((chunks, own_rows, 2 * rows), f32),
+            pltpu.VMEM((2, chunks, rows, depth), bf16),
+            pltpu.VMEM((2, chunks, rows, width), bf16),
+            pltpu.VMEM((2, n_pw, tall, wide), f32),
+            pltpu.VMEM((chunks, n_pw, tall, wide), bf16),
+            pltpu.VMEM((chunks, n_pw, tall, wide), bf16),
+            pltpu.VMEM((chunks, n_pw, tall, wide), bf16),
+            pltpu.VMEM((chunks, n_pw, tall, wide), bf16),
+            pltpu.VMEM((chunks, tall, wide), f32),
             dma((2,)),
             dma((2,)),
             dma((chunks,)),
             dma((chunks,)),
             dma((chunks,)),
-            dma((chunks, 2)),
+            dma((2, chunks)),
             dma((chunks, n_pw)),
             dma((chunks, n_pw)),
             dma((chunks, n_pw)),
@@ -311,7 +357,7 @@
             transcendentals=0,
         ),
         name="kernel_blocks",
-    )(res_pair, band_pair, coulomb[None, :], screening[None, :], forms, res_bands, band_bands)
+    )(res_pair, band_pair, coulomb[None, :], screening[None, :], val_form, cond_form, res_bands, band_bands)
 
 
 def solution(mesh):

time: 79.2 us -> 70.2 us (0.89)
  Pallas kernels: 74.2 us -> 67 us
  other arithmetic: 2.44 us -> 0 us
    pallas_call x1, Pallas kernels: 74.2 us -> 67 us  [local(): pl.pallas_call(functools.partial(kernel, n_blk, n_pw), out_shape=jax.Shap...]
    concatenate x1 -> x0, other arithmetic: 2.44 us -> none  [local(): jnp.concatenate([val_form, cond_form, jnp.zeros((spare, width), val_form....]
where the time goes in v2:
time: 70.2 us; the launch traced here: 69.3 us
  Pallas kernels  67 us (95%)
  local copies, waits for them, and re-layouts  2.26 us (3%)
    pallas_call x1, Pallas kernels, local(): pl.pallas_call(functools.partial(kernel, n_blk, n_pw), out_shape=jax.Shap...  67 us
    unnamed x1, local copies, waits for them, and re-layouts  2.26 us

profile of v2, /device:TPU:0, one launch (start us, length us, event | category | flops | bytes accessed | tf_op | source)
XLA Modules:
  0.0 69.3 jit_solution(5676995389647186526)
XLA Ops:
  0.0 67.0 %kernel_blocks.1 = f32[2,512,256]{2,1,0:T(8,128)} custom-call(bf16[2048,3072]{1,0:T(8,128)(2,1)} %res_hbm.1, bf16[256,3072]{1,0:T(8,128)(2,1)} %band_ref.1, f32[1,3072]{1,0:T(1,128)} %bitcast.2, f32[1,512]{1,0:T(1,128)} %bitcast.3, bf16[400,512]{1,0:T(8,128)(2,1)} %val_form.1, bf16[600,512]{1,0:T(8,128)(2,1)} %cond_form.1, s32[3,2048]{1,0:T(4,128)} %res_bands.1, ...), custom_call_target="tpu_custom_call" | custom-call | flops 7516192768 | bytes 12582912 | tf_op jit(solution)/shard_map/kernel_blocks/pallas_call | solution.py:318
  67.0 2.3 %copy.10 = f32[2,512,256]{2,1,0:T(8,128)} copy(f32[2,512,256]{2,1,0:T(8,128)} %kernel_blocks.1) | data formatting | bytes 2097152

commit v3 on v2

--- a/solution.py
+++ b/solution.py
@@ -307,7 +307,7 @@
     n_band = band_pair.shape[0]
     width = val_form.shape[1]
     n_val, n_cond = val_form.shape[0], cond_form.shape[0]
-    chunks = 4 if n_pw <= 4 else 2
+    chunks = 8 if n_pw <= 4 else 2
     rows = n_band // chunks
     own_rows = n_res // n_pw
     fold = max(1, LANES // (2 * rows))

time: 70.2 us -> 91.6 us (1.30)
  Pallas kernels: 67 us -> 89.1 us
    pallas_call x1, Pallas kernels: 67 us -> 89.1 us  [local(): pl.pallas_call(functools.partial(kernel, n_blk, n_pw), out_shape=jax.Shap...]
where the time goes in v3:
time: 91.6 us; the launch traced here: 91.4 us
  Pallas kernels  89.1 us (97%)
  local copies, waits for them, and re-layouts  2.26 us (2%)
    pallas_call x1, Pallas kernels, local(): pl.pallas_call(functools.partial(kernel, n_blk, n_pw), out_shape=jax.Shap...  89.1 us
    unnamed x1, local copies, waits for them, and re-layouts  2.26 us

profile of v3, /device:TPU:0, one launch (start us, length us, event | category | flops | bytes accessed | tf_op | source)
XLA Modules:
  0.0 91.4 jit_solution(6344393653814922237)
XLA Ops:
  0.0 89.1 %kernel_blocks.1 = f32[2,512,256]{2,1,0:T(8,128)} custom-call(bf16[2048,3072]{1,0:T(8,128)(2,1)} %res_hbm.1, bf16[256,3072]{1,0:T(8,128)(2,1)} %band_ref.1, f32[1,3072]{1,0:T(1,128)} %bitcast.2, f32[1,512]{1,0:T(1,128)} %bitcast.3, bf16[400,512]{1,0:T(8,128)(2,1)} %val_form.1, bf16[600,512]{1,0:T(8,128)(2,1)} %cond_form.1, s32[3,2048]{1,0:T(4,128)} %res_bands.1, ...), custom_call_target="tpu_custom_call" | custom-call | flops 7516192768 | bytes 12582912 | tf_op jit(solution)/shard_map/kernel_blocks/pallas_call | solution.py:318
  89.1 2.3 %copy.10 = f32[2,512,256]{2,1,0:T(8,128)} copy(f32[2,512,256]{2,1,0:T(8,128)} %kernel_blocks.1) | data formatting | bytes 2097152

commit v4 on v2

--- a/solution.py
+++ b/solution.py
@@ -22,7 +22,7 @@
 def kernel(
     n_blk, n_pw,
     res_hbm, band_ref, coul_ref, scr_ref, val_form, cond_form, res_bands, band_bands, out_ref,
-    res, res_sem, val_pad, cond_pad, dens, bidx, idx_in, wgt, rhs, rhs_scr, part, up_in, dn_in, up_out, dn_out, final,
+    res, res_sem, val_pad, cond_pad, dens, bidx, idx_in, wgt, rhs, rhs_scr, turned, part, up_in, dn_in, up_out, dn_out, final,
     idx_send, idx_recv, near_send, far_send, fwd_send, rhs_recv,
     up_send, up_recv, dn_send, dn_recv,
 ):
@@ -167,19 +167,17 @@
             forward(c).start()
 
         landed(*second)
-        weighted = jnp.concatenate([rhs[first], rhs[second]], axis=0)
-        screened = jnp.concatenate([rhs_scr[first], rhs_scr[second]], axis=0)
+        depth = rhs.shape[3]
+        turned[:depth, :] = jnp.concatenate([rhs[first], rhs[second]], axis=0).T
+        turned[depth:, :] = jnp.concatenate([rhs_scr[first], rhs_scr[second]], axis=0).T
 
         @pl.loop(0, n_pw)
         def _(j):
             q = jnp.where(2 * w < n_pw, n_pw - 1 - j, j)
             at = pl.ds(pl.multiple_of(q * own_rows, own_rows), own_rows)
-            contract = (((1,), (1,)), ((), ()))
-            term = lax.dot_general(
-                res[at, :], weighted, contract, preferred_element_type=jnp.float32
-            ) + lax.dot_general(
-                dens[at, :], screened, contract, preferred_element_type=jnp.float32
-            )
+            term = jnp.dot(
+                res[at, :], turned[:depth, :], preferred_element_type=jnp.float32
+            ) + jnp.dot(dens[at, :], turned[depth:, :], preferred_element_type=jnp.float32)
             term = packed(term)
             part[lax.rem(c, 2), q] = term
 
@@ -331,6 +329,7 @@
             pltpu.VMEM((chunks, rows, depth), bf16),
             pltpu.VMEM((2, chunks, rows, depth), bf16),
             pltpu.VMEM((2, chunks, rows, width), bf16),
+            pltpu.VMEM((depth + width, 2 * rows), bf16),
             pltpu.VMEM((2, n_pw, tall, wide), f32),
             pltpu.VMEM((chunks, n_pw, tall, wide), bf16),
             pltpu.VMEM((chunks, n_pw, tall, wide), bf16),

time: 70.2 us -> 71.7 us (1.021)
  Pallas kernels: 67 us -> 68.5 us
    pallas_call x1, Pallas kernels: 67 us -> 68.5 us  [local(): pl.pallas_call(functools.partial(kernel, n_blk, n_pw), out_shape=jax.Shap...]
where the time goes in v4:
time: 71.7 us; the launch traced here: 70.8 us
  Pallas kernels  68.5 us (96%)
  local copies, waits for them, and re-layouts  2.26 us (3%)
    pallas_call x1, Pallas kernels, local(): pl.pallas_call(functools.partial(kernel, n_blk, n_pw), out_shape=jax.Shap...  68.5 us
    unnamed x1, local copies, waits for them, and re-layouts  2.26 us

profile of v4, /device:TPU:0, one launch (start us, length us, event | category | flops | bytes accessed | tf_op | source)
XLA Modules:
  0.0 70.8 jit_solution(10454435938466805839)
XLA Ops:
  0.0 68.5 %kernel_blocks.1 = f32[2,512,256]{2,1,0:T(8,128)} custom-call(bf16[2048,3072]{1,0:T(8,128)(2,1)} %res_hbm.1, bf16[256,3072]{1,0:T(8,128)(2,1)} %band_ref.1, f32[1,3072]{1,0:T(1,128)} %bitcast.2, f32[1,512]{1,0:T(1,128)} %bitcast.3, bf16[400,512]{1,0:T(8,128)(2,1)} %val_form.1, bf16[600,512]{1,0:T(8,128)(2,1)} %cond_form.1, s32[3,2048]{1,0:T(4,128)} %res_bands.1, ...), custom_call_target="tpu_custom_call" | custom-call | flops 7516192768 | bytes 12582912 | tf_op jit(solution)/shard_map/kernel_blocks/pallas_call | solution.py:316
  68.6 2.3 %copy.10 = f32[2,512,256]{2,1,0:T(8,128)} copy(f32[2,512,256]{2,1,0:T(8,128)} %kernel_blocks.1) | data formatting | bytes 2097152

commit v5 on v2

--- a/solution.py
+++ b/solution.py
@@ -158,17 +158,20 @@
         tall = own_rows // fold
         return jnp.concatenate([term[f * tall:(f + 1) * tall] for f in range(fold)], axis=1)
 
-    def multiply(c):
-        first, second = parts_of(c)
-        landed(*first)
-
-        @pl.when(even)
-        def _():
-            forward(c).start()
-
-        landed(*second)
-        weighted = jnp.concatenate([rhs[first], rhs[second]], axis=0)
-        screened = jnp.concatenate([rhs_scr[first], rhs_scr[second]], axis=0)
+    def multiply(group):
+        places = []
+        for c in group:
+            first, second = parts_of(c)
+            landed(*first)
+
+            @pl.when(even)
+            def _():
+                forward(c).start()
+
+            landed(*second)
+            places += [first, second]
+        weighted = jnp.concatenate([rhs[place] for place in places], axis=0)
+        screened = jnp.concatenate([rhs_scr[place] for place in places], axis=0)
 
         @pl.loop(0, n_pw)
         def _(j):
@@ -180,18 +183,23 @@
             ) + lax.dot_general(
                 dens[at, :], screened, contract, preferred_element_type=jnp.float32
             )
-            term = packed(term)
-            part[lax.rem(c, 2), q] = term
+            terms = [
+                packed(term[:, k * 2 * rows:(k + 1) * 2 * rows]) for k in range(len(group))
+            ]
+            for c, piece in zip(group, terms):
+                part[c, q] = piece
 
             @pl.when(jnp.logical_and(w == 0, q > 0))
             def _():
-                up_out[c, q] = term.astype(jnp.bfloat16)
-                send_up(c, q).start()
+                for c, piece in zip(group, terms):
+                    up_out[c, q] = piece.astype(jnp.bfloat16)
+                    send_up(c, q).start()
 
             @pl.when(jnp.logical_and(w == n_pw - 1, q < n_pw - 1))
             def _():
-                dn_out[c, q] = term.astype(jnp.bfloat16)
-                send_dn(c, q).start()
+                for c, piece in zip(group, terms):
+                    dn_out[c, q] = piece.astype(jnp.bfloat16)
+                    send_dn(c, q).start()
 
     def upward(c):
         @pl.when(w > 0)
@@ -200,7 +208,7 @@
             def _(j):
                 q = n_pw - 1 - j
                 send_up(c, q).wait_recv()
-                total = part[lax.rem(c, 2), q] + up_in[c, q].astype(jnp.float32)
+                total = part[c, q] + up_in[c, q].astype(jnp.float32)
                 up_out[c, q] = total.astype(jnp.bfloat16)
                 send_up(c, q).start()
 
@@ -210,7 +218,7 @@
             @pl.loop(0, w)
             def _(q):
                 send_dn(c, q).wait_recv()
-                total = part[lax.rem(c, 2), q] + dn_in[c, q].astype(jnp.float32)
+                total = part[c, q] + dn_in[c, q].astype(jnp.float32)
                 dn_out[c, q] = total.astype(jnp.bfloat16)
                 send_dn(c, q).start()
 
@@ -232,7 +240,7 @@
         def _():
             upward(c)
 
-        final[c] = part[lax.rem(c, 2), w]
+        final[c] = part[c, w]
 
         @pl.when(w > 0)
         def _():
@@ -244,16 +252,17 @@
             send_dn(c, w).wait_recv()
             final[c] += dn_in[c, w].astype(jnp.float32)
 
-    @pl.loop(0, chunks)
-    def _(c):
-        multiply(c)
-        relay_near_end(c)
-
-        @pl.when(c > 0)
-        def _():
-            relay_rest(c - 1)
-
-    relay_rest(chunks - 1)
+    groups = [(0, 1)] + [(c,) for c in range(2, chunks)]
+    late = []
+    for group in groups:
+        multiply(group)
+        for c in group:
+            relay_near_end(c)
+        for c in late:
+            relay_rest(c)
+        late = group
+    for c in late:
+        relay_rest(c)
 
     tall = final.shape[1]
 
@@ -331,7 +340,7 @@
             pltpu.VMEM((chunks, rows, depth), bf16),
             pltpu.VMEM((2, chunks, rows, depth), bf16),
             pltpu.VMEM((2, chunks, rows, width), bf16),
-            pltpu.VMEM((2, n_pw, tall, wide), f32),
+            pltpu.VMEM((chunks, n_pw, tall, wide), f32),
             pltpu.VMEM((chunks, n_pw, tall, wide), bf16),
             pltpu.VMEM((chunks, n_pw, tall, wide), bf16),
             pltpu.VMEM((chunks, n_pw, tall, wide), bf16),

time: 70.2 us -> 69.8 us (level)
  no operation moved by 1% of the time
where the time goes in v5:
time: 69.8 us; the launch traced here: 69.6 us
  Pallas kernels  67.3 us (96%)
  local copies, waits for them, and re-layouts  2.26 us (3%)
    pallas_call x1, Pallas kernels, local(): pl.pallas_call(functools.partial(kernel, n_blk, n_pw), out_shape=jax.Shap...  67.3 us
    unnamed x1, local copies, waits for them, and re-layouts  2.26 us

profile of v5, /device:TPU:0, one launch (start us, length us, event | category | flops | bytes accessed | tf_op | source)
XLA Modules:
  0.0 69.6 jit_solution(3097815952667201585)
XLA Ops:
  0.0 67.3 %kernel_blocks.1 = f32[2,512,256]{2,1,0:T(8,128)} custom-call(bf16[2048,3072]{1,0:T(8,128)(2,1)} %res_hbm.1, bf16[256,3072]{1,0:T(8,128)(2,1)} %band_ref.1, f32[1,3072]{1,0:T(1,128)} %bitcast.2, f32[1,512]{1,0:T(1,128)} %bitcast.3, bf16[400,512]{1,0:T(8,128)(2,1)} %val_form.1, bf16[600,512]{1,0:T(8,128)(2,1)} %cond_form.1, s32[3,2048]{1,0:T(4,128)} %res_bands.1, ...), custom_call_target="tpu_custom_call" | custom-call | flops 7516192768 | bytes 12582912 | tf_op jit(solution)/shard_map/kernel_blocks/pallas_call | solution.py:327
  67.3 2.3 %copy.10 = f32[2,512,256]{2,1,0:T(8,128)} copy(f32[2,512,256]{2,1,0:T(8,128)} %kernel_blocks.1) | data formatting | bytes 2097152

commit v6 on v5

--- a/solution.py
+++ b/solution.py
@@ -122,11 +122,18 @@
         )
         return (valence * conduct).astype(jnp.bfloat16)
 
-    @pl.loop(0, dens.shape[0] // GROUP)
-    def _(g):
+    def fill(g):
         at = pl.ds(pl.multiple_of(g * GROUP, GROUP), GROUP)
         point = res_bands[2:3, at]
         dens[at, :] = density(point * NV + res_bands[0:1, at], point * NC + res_bands[1:2, at])
+
+    by_block = own_rows % GROUP == 0
+
+    @pl.when(even if by_block else me >= 0)
+    def _():
+        @pl.loop(0, dens.shape[0] // GROUP)
+        def _(g):
+            fill(g)
 
     for slot, target in ((0, one_on), (1, two_on)):
         send_index(slot, target).wait_recv()
@@ -177,6 +184,13 @@
         def _(j):
             q = jnp.where(2 * w < n_pw, n_pw - 1 - j, j)
             at = pl.ds(pl.multiple_of(q * own_rows, own_rows), own_rows)
+            if by_block and group[0] == 0:
+                @pl.when(jnp.logical_not(even))
+                def _():
+                    @pl.loop(0, own_rows // GROUP)
+                    def _(g):
+                        fill(q * (own_rows // GROUP) + g)
+
             contract = (((1,), (1,)), ((), ()))
             term = lax.dot_general(
                 res[at, :], weighted, contract, preferred_element_type=jnp.float32

time: 69.8 us -> 69.8 us (level)
  no operation moved by 1% of the time
where the time goes in v6:
time: 69.8 us; the launch traced here: 69.6 us
  Pallas kernels  67.3 us (96%)
  local copies, waits for them, and re-layouts  2.26 us (3%)
    pallas_call x1, Pallas kernels, local(): pl.pallas_call(functools.partial(kernel, n_blk, n_pw), out_shape=jax.Shap...  67.3 us
    unnamed x1, local copies, waits for them, and re-layouts  2.26 us

profile of v6, /device:TPU:0, one launch (start us, length us, event | category | flops | bytes accessed | tf_op | source)
XLA Modules:
  0.0 69.6 jit_solution(14009006126336324184)
XLA Ops:
  0.0 67.3 %kernel_blocks.1 = f32[2,512,256]{2,1,0:T(8,128)} custom-call(bf16[2048,3072]{1,0:T(8,128)(2,1)} %res_hbm.1, bf16[256,3072]{1,0:T(8,128)(2,1)} %band_ref.1, f32[1,3072]{1,0:T(1,128)} %bitcast.2, f32[1,512]{1,0:T(1,128)} %bitcast.3, bf16[400,512]{1,0:T(8,128)(2,1)} %val_form.1, bf16[600,512]{1,0:T(8,128)(2,1)} %cond_form.1, s32[3,2048]{1,0:T(4,128)} %res_bands.1, ...), custom_call_target="tpu_custom_call" | custom-call | flops 7516192768 | bytes 12582912 | tf_op jit(solution)/shard_map/kernel_blocks/pallas_call | solution.py:341
  67.3 2.3 %copy.10 = f32[2,512,256]{2,1,0:T(8,128)} copy(f32[2,512,256]{2,1,0:T(8,128)} %kernel_blocks.1) | data formatting | bytes 2097152

commit v7 on v5

--- a/solution.py
+++ b/solution.py
@@ -252,7 +252,7 @@
             send_dn(c, w).wait_recv()
             final[c] += dn_in[c, w].astype(jnp.float32)
 
-    groups = [(0, 1)] + [(c,) for c in range(2, chunks)]
+    groups = [(0, 1, 2, 3), (4, 5, 6), (7,)] if chunks == 8 else [tuple(range(chunks))]
     late = []
     for group in groups:
         multiply(group)
@@ -316,7 +316,7 @@
     n_band = band_pair.shape[0]
     width = val_form.shape[1]
     n_val, n_cond = val_form.shape[0], cond_form.shape[0]
-    chunks = 4 if n_pw <= 4 else 2
+    chunks = 8 if n_pw <= 4 else 2
     rows = n_band // chunks
     own_rows = n_res // n_pw
     fold = max(1, LANES // (2 * rows))

time: 69.8 us -> 74.4 us (1.066)
  Pallas kernels: 67.3 us -> 72 us
    pallas_call x1, Pallas kernels: 67.3 us -> 72 us  [local(): pl.pallas_call(functools.partial(kernel, n_blk, n_pw), out_shape=jax.Shap...]
where the time goes in v7:
time: 74.4 us; the launch traced here: 74.2 us
  Pallas kernels  72 us (97%)
  local copies, waits for them, and re-layouts  2.26 us (3%)
    pallas_call x1, Pallas kernels, local(): pl.pallas_call(functools.partial(kernel, n_blk, n_pw), out_shape=jax.Shap...  72 us
    unnamed x1, local copies, waits for them, and re-layouts  2.26 us

profile of v7, /device:TPU:0, one launch (start us, length us, event | category | flops | bytes accessed | tf_op | source)
XLA Modules:
  0.0 74.2 jit_solution(1827243091821805115)
XLA Ops:
  0.0 72.0 %kernel_blocks.1 = f32[2,512,256]{2,1,0:T(8,128)} custom-call(bf16[2048,3072]{1,0:T(8,128)(2,1)} %res_hbm.1, bf16[256,3072]{1,0:T(8,128)(2,1)} %band_ref.1, f32[1,3072]{1,0:T(1,128)} %bitcast.2, f32[1,512]{1,0:T(1,128)} %bitcast.3, bf16[400,512]{1,0:T(8,128)(2,1)} %val_form.1, bf16[600,512]{1,0:T(8,128)(2,1)} %cond_form.1, s32[3,2048]{1,0:T(4,128)} %res_bands.1, ...), custom_call_target="tpu_custom_call" | custom-call | flops 7516192768 | bytes 12582912 | tf_op jit(solution)/shard_map/kernel_blocks/pallas_call | solution.py:327
  72.0 2.3 %copy.10 = f32[2,512,256]{2,1,0:T(8,128)} copy(f32[2,512,256]{2,1,0:T(8,128)} %kernel_blocks.1) | data formatting | bytes 2097152
